TPU v7x, 256 devices: a whole 4x4x8 slice. The times are simulated.
256 devices in a mesh: comp: 2 (over core), gx: 16 (over x, z_hi), gy: 8 (over z_lo, y).
Axes of the slice: x: 4, y: 4, z: 8 (z_hi: 4, z_lo: 2; z = z_hi * 2 + z_lo), core: 2. Of those that a mesh axis runs over, the one named last changes fastest.
Arguments:
- final_adjoint: float32 [2, 128, 512, 1024], P('comp', None, 'gx', 'gy'), may hold values from -6 to 6
- innovations: float32 [4, 2, 32768, 128], P(None, 'comp', ('gx', 'gy')), may hold values from -6 to 6
- obs_owner: int32 [4, 2, 32768, 1], P(None, 'comp', ('gx', 'gy')), may hold values from 0 to 127; in each aligned block of 256 rows (0 to 255, 256 to 511, ..., all dimensions but the last counted through in order) at most 4 rows name the same one
- obs_column: int32 [4, 2, 32768], P(None, 'comp', ('gx', 'gy')), may hold values from 0 to 4095
- coupler: int32 [4, 2, 512, 1024], P(None, 'comp', 'gx', 'gy'), may hold values from 0 to 4095
- sea_mask: int32 [512, 1024], P('gx', 'gy'), may hold values 0 or 1
- diffusion: float32 [2, 128], P('comp'), may hold values from 0.02 to 0.24
- vertical: float32 [2, 128, 128], P('comp'), may hold values from -0.5 to 0.5
- flux_out: float32 [2, 5, 128], P('comp'), may hold values from -0.5 to 0.5
- flux_in: float32 [2, 128, 5], P('comp'), may hold values from -1.25 to 1.25
Outputs:
- start_adjoint: float32 [2, 128, 512, 1024], P('comp', None, 'gx', 'gy')
Inputs may be any that keep to these rules, and one draw needn't show every extreme that they name: `obs_owner`: among the 256 profiles of one device, one step and one component, no tile is named more than 4 times, a bound that some block reaches.
All inputs are finite; a program needn't handle non-finite values. No bound on the sum of `sea_mask` on one device may be relied on, other than what follows from the above.
Results may differ from a plain program's by a relative error of at most 0.0001.
Values sent between devices are 32-bit elements; how exact they have to be, the bound alone decides.
A program may use at most 64 MiB of HBM per device.

v0:
```python
import jax
import jax.numpy as jnp
from jax import lax
from jax.experimental import pallas as pl
from jax.experimental.pallas import tpu as pltpu
from jax.sharding import PartitionSpec as P

MESH = pl.DeviceIdType.MESH
STEPS = 4
ROWS = 32
COLS = 128
LEV = 128
PROF = 256
SLOTS = 512
FIELDS = 5
HALF = ROWS // 2
BF = jnp.bfloat16
F32 = jnp.float32
I32 = jnp.int32

NN = (((1,), (0,)), ((), ()))
NT = (((1,), (1,)), ((), ()))
TN = (((0,), (0,)), ((), ()))


def dot(a, b, dims):
    return lax.dot_general(a, b, dims, preferred_element_type=F32)


def halves(value):
    high = value.astype(BF)
    low = (value - high.astype(F32)).astype(BF)
    return high, low


def at_chip(x, y, z):
    return {"gx": x * 4 + z // 2, "gy": lax.rem(z, 2) * 4 + y}


def kernel(
    state_hbm,
    innov_hbm,
    owner_ref,
    column_ref,
    coupler_ref,
    mask_ref,
    diff_ref,
    vert_ref,
    fout_ref,
    fin_ref,
    out_hbm,
    grid_in,
    innov,
    ext,
    send_buf,
    mid_buf,
    prof_buf,
    state_hl,
    mask_full,
    onehot,
    prof_hl,
    col_send,
    col_mid,
    col_line,
    col_recv,
    col_wide,
    col_rows,
    surf,
    partner,
    received,
    weights,
    weights_t,
    surf_w,
    fin_w,
    fin_wt,
    small,
    load_sem,
    s1,
    r1,
    l1,
    s2,
    r2,
    l2,
    col_sem,
    halo_s,
    halo_r,
    part_s,
    part_r,
    out_sem,
):
    comp = lax.axis_index("comp")
    gx = lax.axis_index("gx")
    gy = lax.axis_index("gy")
    x, y = gx // 4, lax.rem(gy, 4)
    z = lax.rem(gx, 4) * 2 + gy // 4
    q = x * 4 + y

    load_innov = pltpu.make_async_copy(innov_hbm, innov, load_sem.at[0])
    load_state = pltpu.make_async_copy(state_hbm, grid_in, load_sem.at[1])
    load_innov.start()
    load_state.start()

    def zero_edges(step, carry):
        ext[step, 0] = jnp.zeros((144, LEV), F32)
        ext[step, ROWS + 1] = jnp.zeros((144, LEV), F32)
        ext[step, 1 : ROWS + 1, 0:8, :] = jnp.zeros((ROWS, 8, LEV), F32)
        ext[step, 1 : ROWS + 1, 136:144, :] = jnp.zeros((ROWS, 8, LEV), F32)
        return carry

    lax.fori_loop(0, STEPS, zero_edges, 0)

    def xy_peer(i):
        return lax.rem(x + i // 4, 4), lax.rem(y + lax.rem(i, 4), 4)

    barrier = pltpu.get_barrier_semaphore()

    def greet(target):
        pl.semaphore_signal(barrier, inc=1, device_id=target, device_id_type=MESH)

    for i in range(1, 16):
        x2, y2 = xy_peer(jnp.int32(i))
        greet(at_chip(x2, y2, z))
    for i in range(1, 8):
        greet(at_chip(x, y, lax.rem(z + i, 8)))
    greet({"comp": 1 - comp})

    sides = (
        (gx > 0, {"gx": gx - 1}),
        (gx < 15, {"gx": gx + 1}),
        (gy > 0, {"gy": gy - 1}),
        (gy < 7, {"gy": gy + 1}),
    )
    for there, target in sides:

        @pl.when(there)
        def _(target=target):
            greet(target)

    greeted = 23
    for there, _ in sides:
        greeted = greeted + jnp.where(there, 1, 0)

    vert = vert_ref[...]
    v_high, v_low = halves(vert)
    weights[0:128, 0:128] = v_high
    weights[128:256, 0:128] = v_high
    weights[0:128, 128:256] = v_low
    weights[128:256, 128:256] = v_low
    vt_high, vt_low = halves(vert.T)
    weights_t[0:128, 0:128] = vt_high
    weights_t[0:128, 128:256] = vt_high
    weights_t[128:256, 0:128] = vt_low
    weights_t[128:256, 128:256] = vt_low
    small[...] = jnp.zeros((16, LEV), F32)
    small[0:FIELDS, :] = fout_ref[...]
    small[8 : 8 + FIELDS, :] = fin_ref[...]
    flux_w = lax.dot_general(
        small[0:8, :], vert, NT, precision=lax.Precision.HIGHEST, preferred_element_type=F32
    )
    g_high = flux_w.astype(BF).astype(F32)
    g_both = jnp.concatenate([g_high, flux_w - g_high], axis=0).astype(BF)
    surf_w[:, 0:128] = g_both
    surf_w[:, 128:256] = g_both
    fin = small[8:16, :]
    f_high = fin.astype(BF).astype(F32)
    f_all = jnp.concatenate([f_high, f_high, fin - f_high, jnp.zeros((8, LEV), F32)], axis=0)
    fin_w[...] = f_all.astype(BF)
    f_pad = jnp.concatenate([f_all, jnp.zeros((96, LEV), F32)], axis=0)
    fin_wt[...] = f_pad.T.astype(BF)
    received[...] = jnp.zeros((ROWS, 8, COLS), F32)

    lane_b = lax.broadcasted_iota(I32, (128, 128), 1)
    sub_b = lax.broadcasted_iota(I32, (128, 128), 0)
    earlier = sub_b < lane_b

    def slot_of(step):
        owner = owner_ref[pl.ds(step, 1), :]
        first, second = owner[:, 0:128], owner[:, 128:256]
        first_b = jnp.broadcast_to(first, (128, 128))
        second_b = jnp.broadcast_to(second, (128, 128))
        first_t = first_b.astype(F32).T.astype(I32)
        second_t = second_b.astype(F32).T.astype(I32)
        one = jnp.where((first_t == first_b) & earlier, 1, 0)
        two = jnp.where(first_t == second_b, 1, 0)
        three = jnp.where((second_t == second_b) & earlier, 1, 0)
        rank = jnp.concatenate(
            [
                jnp.sum(one, axis=0, keepdims=True),
                jnp.sum(two + three, axis=0, keepdims=True),
            ],
            axis=1,
        )
        owner_q = (owner >> 5) * 4 + (owner & 3)
        owner_z = ((owner >> 3) & 3) * 2 + ((owner >> 2) & 1)
        return owner_q, owner_z, rank

    def pack(step):
        owner_q, owner_z, rank = slot_of(step)
        slot = (owner_q * 8 + owner_z) * 4 + rank
        placing = jnp.where(
            jnp.broadcast_to(slot, (SLOTS, PROF)) == lax.broadcasted_iota(I32, (SLOTS, PROF), 0),
            1.0,
            0.0,
        ).astype(BF)
        high, low = halves(innov[step])
        placed = dot(placing, jnp.concatenate([high, low], axis=1), NN)
        send_buf[step] = (placed[:, 0:LEV] + placed[:, LEV:]).reshape(16, 32, LEV)
        columns = column_ref[pl.ds(step, 1), :]
        to_q = jnp.broadcast_to(owner_q, (16, PROF)) == lax.broadcasted_iota(I32, (16, PROF), 0)
        row_part = jnp.where(to_q, (columns >> 7).astype(F32), 0.0)
        col_part = jnp.where(to_q, (columns & 127).astype(F32), 0.0)
        both = jnp.concatenate([row_part, col_part], axis=0).astype(BF)
        lane = owner_z * 16 + step * 4 + rank
        spread = jnp.where(
            jnp.broadcast_to(lane, (128, PROF)) == lax.broadcasted_iota(I32, (128, PROF), 0),
            1.0,
            0.0,
        ).astype(BF)
        lines = dot(both, spread, NT)
        return lines[0:16] * 128.0 + lines[16:32]

    def first_leg(step):
        pltpu.make_async_copy(send_buf.at[step, q], mid_buf.at[step, q], l1.at[step]).start()

        def send(i, carry):
            x2, y2 = xy_peer(i)
            pltpu.make_async_remote_copy(
                send_buf.at[step, x2 * 4 + y2],
                mid_buf.at[step, q],
                s1.at[step],
                r1.at[step],
                device_id=at_chip(x2, y2, z),
                device_id_type=MESH,
            ).start()
            return carry

        lax.fori_loop(1, 16, send, 0)

    def many(ref, sem):
        return pltpu.make_async_copy(ref, ref, sem)

    def second_leg(step):
        pltpu.make_async_copy(send_buf.at[step, q], mid_buf.at[step, q], l1.at[step]).wait()
        many(mid_buf.at[step, pl.ds(0, 15)], r1.at[step]).wait()

        def block(z2):
            return mid_buf.at[step, :, pl.ds(pl.multiple_of(z2 * 4, 4), 4), :]

        pltpu.make_async_copy(block(z), prof_buf.at[step, z], l2.at[step]).start()

        def send(i, carry):
            z2 = lax.rem(z + i, 8)
            pltpu.make_async_remote_copy(
                block(z2),
                prof_buf.at[step, z],
                s2.at[step],
                r2.at[step],
                device_id=at_chip(x, y, z2),
                device_id_type=MESH,
            ).start()
            return carry

        lax.fori_loop(1, 8, send, 0)

    def arrived(step):
        pltpu.make_async_copy(
            mid_buf.at[step, :, pl.ds(0, 4), :], prof_buf.at[step, z], l2.at[step]
        ).wait()
        many(prof_buf.at[step, pl.ds(0, 7)], r2.at[step]).wait()

    load_innov.wait()
    lines = pack(3)
    pl.semaphore_wait(barrier, greeted)
    first_leg(3)
    for step in (2, 1, 0):
        lines = lines + pack(step)
        first_leg(step)
    col_send[...] = jnp.broadcast_to(lines[:, None, :], (16, 8, LEV))
    col_mid[pl.ds(q, 1)] = col_send[pl.ds(q, 1)]

    def send_columns(i, carry):
        x2, y2 = xy_peer(i)
        pltpu.make_async_remote_copy(
            col_send.at[x2 * 4 + y2],
            col_mid.at[q],
            col_sem.at[0],
            col_sem.at[1],
            device_id=at_chip(x2, y2, z),
            device_id_type=MESH,
        ).start()
        return carry

    lax.fori_loop(1, 16, send_columns, 0)
    second_leg(3)

    load_state.wait()

    def turn(i, carry):
        for u in range(4):
            r = i * 4 + u
            ext[3, r + 1, 8:136, :] = grid_in[pl.ds(r, LEV, stride=ROWS), :].T
        return carry

    lax.fori_loop(0, ROWS // 4, turn, 0)

    many(col_mid.at[pl.ds(0, 15)], col_sem.at[1]).wait()
    col_line[...] = col_mid[:, 0, :]
    col_recv[pl.ds(z, 1)] = col_line[...][None]

    def send_lines(i, carry):
        z2 = lax.rem(z + i, 8)
        pltpu.make_async_remote_copy(
            col_line,
            col_recv.at[z],
            col_sem.at[2],
            col_sem.at[3],
            device_id=at_chip(x, y, z2),
            device_id_type=MESH,
        ).start()
        return carry

    lax.fori_loop(1, 8, send_lines, 0)
    second_leg(2)

    is_ocean = comp == 0

    def spread_mask(i, carry):
        for u in range(4):
            r = i * 4 + u
            line = jnp.where(is_ocean, mask_ref[pl.ds(r, 1), :].astype(F32), 1.0)
            mask_full[r] = jnp.broadcast_to(line, (COLS, COLS)).T
        return carry

    lax.fori_loop(0, ROWS // 4, spread_mask, 0)

    many(col_recv.at[pl.ds(0, 7)], col_sem.at[3]).wait()
    came = col_recv[...].reshape(128, 128)
    came_row = jnp.floor(came * (1.0 / 128.0))
    came_col = came - came_row * 128.0
    source = lax.broadcasted_iota(I32, (128, SLOTS), 0)
    repeat = jnp.where(source == (lax.broadcasted_iota(I32, (128, SLOTS), 1) >> 2), 1.0, 0.0).astype(BF)
    own_slot = (lax.broadcasted_iota(I32, (16, SLOTS), 0) & 3) == (
        lax.broadcasted_iota(I32, (16, SLOTS), 1) & 3
    )
    for part, value in enumerate((came_row, came_col)):
        col_wide[...] = dot(value.astype(BF), repeat, TN)
        mine = col_wide[pl.ds(pl.multiple_of(z * 16, 16), 16), :]
        mine = jnp.where(own_slot, mine, 0.0)
        for step in range(STEPS):
            col_rows[part, step : step + 1, :] = jnp.sum(
                mine[step * 4 : step * 4 + 4], axis=0, keepdims=True
            )

    def chunk_rows(i):
        return pl.ds(1 + i * HALF, HALF)

    def scatter(step):
        high, low = halves(prof_buf[step].reshape(SLOTS, LEV))
        prof_hl[:, 0:LEV] = high
        prof_hl[:, LEV:] = low
        rows_id = col_rows[0, step : step + 1, :]
        cols_id = col_rows[1, step : step + 1, :]
        cell = lax.broadcasted_iota(I32, (COLS, SLOTS), 0).astype(F32).astype(BF)

        def chunk(i, carry):
            for u in range(HALF):
                r = (i * HALF + u).astype(F32)
                wanted = jnp.where(rows_id == r, cols_id, -1.0)
                wanted = jnp.broadcast_to(wanted, (16, SLOTS)).astype(BF)
                wanted = jnp.concatenate([wanted] * 8, axis=0)
                onehot[u * COLS : (u + 1) * COLS, :] = jnp.where(wanted == cell, BF(1), BF(0))
            added = dot(onehot[...], prof_hl[...], NN)
            added = (added[:, 0:LEV] + added[:, LEV:]).reshape(HALF, COLS, LEV)
            ext[step, chunk_rows(i), 8:136, :] = ext[step, chunk_rows(i), 8:136, :] + added
            return carry

        lax.fori_loop(0, 2, chunk, 0)

    def halo_copy(step, side):
        row, col = pl.ds(8, COLS), pl.ds(1, ROWS)
        src, dst = (
            (ext.at[step, 1, row], ext.at[step, ROWS + 1, row]),
            (ext.at[step, ROWS, row], ext.at[step, 0, row]),
            (ext.at[step, col, pl.ds(8, 1)], ext.at[step, col, pl.ds(136, 1)]),
            (ext.at[step, col, pl.ds(135, 1)], ext.at[step, col, pl.ds(7, 1)]),
        )[side]
        return pltpu.make_async_remote_copy(
            src,
            dst,
            halo_s.at[step, side],
            halo_r.at[step, side],
            device_id=sides[side][1],
            device_id_type=MESH,
        )

    def halo_start(step):
        for side in range(4):

            @pl.when(sides[side][0])
            def _(side=side):
                halo_copy(step, side).start()

    def halo_wait(step):
        for side in range(4):

            @pl.when(sides[side][0])
            def _(side=side):
                halo_copy(step, side).wait_send()
                halo_copy(step, side ^ 1).wait_recv()

    def stencil(step):
        rate = diff_ref[0:1, :]
        rest = 1.0 - 4.0 * rate

        def rows(i, carry):
            for u in range(4):
                r = i * 4 + u
                here = ext[step, r + 1, 8:136, :]
                beside = (
                    ext[step, r, 8:136, :]
                    + ext[step, r + 2, 8:136, :]
                    + ext[step, r + 1, 7:135, :]
                    + ext[step, r + 1, 9:137, :]
                )
                value = (here * rest + beside * rate) * mask_full[r]
                high, low = halves(value)
                at = pl.ds(pl.multiple_of(r * COLS, COLS), COLS)
                state_hl[at, 0:LEV] = high
                state_hl[at, LEV:] = low
            return carry

        lax.fori_loop(0, ROWS // 4, rows, 0)

    def chunk_cells(i):
        return pl.ds(pl.multiple_of(i * HALF * COLS, HALF * COLS), HALF * COLS)

    def surfaces(step):
        def chunk(i, carry):
            both = dot(surf_w[...], state_hl[chunk_cells(i), :], NT)
            total = both[0:8] + both[8:16]
            for j in range(HALF):
                surf[step, i * HALF + j] = total[:, j * COLS : (j + 1) * COLS]
            return carry

        lax.fori_loop(0, 2, chunk, 0)

    def partner_copy(step):
        return pltpu.make_async_remote_copy(
            surf.at[step],
            partner.at[step],
            part_s.at[step],
            part_r.at[step],
            device_id={"comp": 1 - comp},
            device_id_type=MESH,
        )

    def vertical(step):
        def chunk(i, carry):
            mixed = dot(state_hl[chunk_cells(i), :], weights[...], NN)
            mixed = mixed[:, 0:LEV] + mixed[:, LEV:]
            ext[step, chunk_rows(i), 8:136, :] = mixed.reshape(HALF, COLS, LEV)
            return carry

        lax.fori_loop(0, 2, chunk, 0)

    def couple(step):
        def block(b, carry):
            index = coupler_ref[step, pl.ds(pl.multiple_of(b * 8, 8), 8), :]
            lane, row = index & 127, index >> 7
            sums = [jnp.zeros((8, COLS), F32) for _ in range(FIELDS)]
            for r in range(ROWS):
                hit = row == r
                for f in range(FIELDS):
                    line = jnp.broadcast_to(partner[step, r, f : f + 1, :], (8, COLS))
                    sums[f] = jnp.where(hit, jnp.take_along_axis(line, lane, axis=1), sums[f])
            for f in range(FIELDS):
                for j in range(8):
                    received[b * 8 + j, f : f + 1, :] = sums[f][j : j + 1, :]
            return carry

        lax.fori_loop(0, 4, block, 0)

    def received_parts(i):
        value = jnp.concatenate([received[i * HALF + j] for j in range(HALF)], axis=1)
        high = value.astype(BF).astype(F32)
        low = value - high
        return jnp.concatenate([high, low, high, low], axis=0).astype(BF)

    def add_fluxes(step):
        def chunk(i, carry):
            added = dot(received_parts(i), fin_w[...], TN).reshape(HALF, COLS, LEV)
            ext[step, chunk_rows(i), 8:136, :] = ext[step, chunk_rows(i), 8:136, :] + added
            return carry

        lax.fori_loop(0, 2, chunk, 0)

    def finish():
        def chunk(i, carry):
            mixed = dot(weights_t[...], state_hl[chunk_cells(i), :], NT)
            mixed = mixed[0:LEV] + mixed[LEV:]
            mixed = mixed + dot(fin_wt[:, 0:32], received_parts(i), NN)
            for j in range(HALF):
                grid_in[pl.ds(i * HALF + j, LEV, stride=ROWS), :] = mixed[
                    :, j * COLS : (j + 1) * COLS
                ]
            return carry

        lax.fori_loop(0, 2, chunk, 0)

    for step in (3, 2, 1, 0):
        if step < 3:
            vertical(step)
        if step == 3:
            second_leg(1)
        arrived(step)
        scatter(step)
        if step < 3:
            partner_copy(step + 1).wait()
            couple(step + 1)
            add_fluxes(step)
        halo_start(step)
        if step == 3:
            second_leg(0)
        halo_wait(step)
        stencil(step)
        surfaces(step)
        partner_copy(step).start()
    partner_copy(0).wait()
    couple(0)
    finish()
    store = pltpu.make_async_copy(grid_in, out_hbm, out_sem)
    store.start()

    many(col_mid.at[pl.ds(0, 15)], col_sem.at[0]).wait()
    many(col_recv.at[pl.ds(0, 7)], col_sem.at[2]).wait()
    for step in range(STEPS):
        many(mid_buf.at[step, pl.ds(0, 15)], s1.at[step]).wait()
        many(prof_buf.at[step, pl.ds(0, 7)], s2.at[step]).wait()
    store.wait()


def body(
    final_adjoint,
    innovations,
    obs_owner,
    obs_column,
    coupler,
    sea_mask,
    diffusion,
    vertical,
    flux_out,
    flux_in,
):
    whole = pl.BlockSpec(memory_space=pl.ANY)
    near = pl.BlockSpec(memory_space=pltpu.VMEM)
    dma = pltpu.SemaphoreType.DMA
    result = pl.pallas_call(
        kernel,
        out_shape=jax.ShapeDtypeStruct((LEV * ROWS, COLS), F32),
        in_specs=[whole, whole] + [near] * 8,
        out_specs=whole,
        scratch_shapes=[
            pltpu.VMEM((LEV * ROWS, COLS), F32),
            pltpu.VMEM((STEPS, PROF, LEV), F32),
            pltpu.VMEM((STEPS, ROWS + 2, 144, LEV), F32),
            pltpu.VMEM((STEPS, 16, 32, LEV), F32),
            pltpu.VMEM((STEPS, 16, 32, LEV), F32),
            pltpu.VMEM((STEPS, 8, 16, 4, LEV), F32),
            pltpu.VMEM((ROWS * COLS, 2 * LEV), BF),
            pltpu.VMEM((ROWS, COLS, LEV), F32),
            pltpu.VMEM((HALF * COLS, SLOTS), BF),
            pltpu.VMEM((SLOTS, 2 * LEV), BF),
            pltpu.VMEM((16, 8, LEV), F32),
            pltpu.VMEM((16, 8, LEV), F32),
            pltpu.VMEM((16, LEV), F32),
            pltpu.VMEM((8, 16, LEV), F32),
            pltpu.VMEM((128, SLOTS), F32),
            pltpu.VMEM((2, STEPS, SLOTS), F32),
            pltpu.VMEM((STEPS, ROWS, 8, COLS), F32),
            pltpu.VMEM((STEPS, ROWS, 8, COLS), F32),
            pltpu.VMEM((ROWS, 8, COLS), F32),
            pltpu.VMEM((256, 256), BF),
            pltpu.VMEM((256, 256), BF),
            pltpu.VMEM((16, 256), BF),
            pltpu.VMEM((32, LEV), BF),
            pltpu.VMEM((LEV, 128), BF),
            pltpu.VMEM((16, LEV), F32),
            dma((2,)),
            dma((STEPS,)),
            dma((STEPS,)),
            dma((STEPS,)),
            dma((STEPS,)),
            dma((STEPS,)),
            dma((STEPS,)),
            dma((4,)),
            dma((STEPS, 4)),
            dma((STEPS, 4)),
            dma((STEPS,)),
            dma((STEPS,)),
            dma,
        ],
        compiler_params=pltpu.CompilerParams(
            collective_id=0, has_side_effects=True, vmem_limit_bytes=52 * 2**20
        ),
    )(
        final_adjoint.reshape(LEV * ROWS, COLS),
        innovations.reshape(STEPS, PROF, LEV),
        obs_owner.reshape(STEPS, PROF),
        obs_column.reshape(STEPS, PROF),
        coupler.reshape(STEPS, ROWS, COLS),
        sea_mask,
        diffusion,
        vertical[0],
        flux_out[0],
        flux_in[0].T,
    )
    return result.reshape(1, LEV, ROWS, COLS)


def solution(mesh):
    placed = (
        P("comp", None, "gx", "gy"),
        P(None, "comp", ("gx", "gy"), None),
        P(None, "comp", ("gx", "gy"), None),
        P(None, "comp", ("gx", "gy")),
        P(None, "comp", "gx", "gy"),
        P("gx", "gy"),
        P("comp", None),
        P("comp", None, None),
        P("comp", None, None),
        P("comp", None, None),
    )
    return jax.shard_map(
        body, mesh=mesh, in_specs=placed, out_specs=P("comp", None, "gx", "gy"), check_vma=False
    )
```

profile of v0, /device:TPU:35, one launch (start us, length us, event | category | flops | bytes accessed | tf_op | source)
XLA Modules:
  0.0 94.4 jit_solution(506259869915198412)
XLA Ops:
  0.0 0.7 copy.22
  0.7 0.7 copy.21
  1.4 0.7 copy.20
  2.1 0.7 copy.19
  2.7 0.0 copy-start
  2.7 1.0 %copy-done = f32[4,1,256,128]{3,2,1,0:T(8,128)S(1)} copy-done((f32[4,1,256,128]{3,2,1,0:T(8,128)S(1)}, f32[4,1,256,128]{3,2,1,0:T(8,128)}, u32[]{:S(2)}) %copy-start) | copy-done | bytes 524312
  3.8 0.0 copy-start.1
  3.8 0.8 copy-done.1
  4.6 0.0 copy-start.2
  4.6 0.8 copy-done.2
  5.5 0.0 copy-start.3
  5.5 0.7 copy-done.3
  6.2 0.0 copy-start.4
  6.2 0.7 copy-done.4
  6.8 84.5 %shard_map.100 = f32[4096,128]{1,0:T(8,128)} custom-call(f32[4096,128]{1,0:T(8,128)} %bitcast.27, f32[4,256,128]{2,1,0:T(8,128)S(1)} %bitcast.19, s32[4,256]{1,0:T(4,128)S(1)} %bitcast.22, s32[4,256]{1,0:T(4,128)S(1)} %bitcast.23, s32[4,32,128]{2,1,0:T(8,128)S(1)} %bitcast.20, s32[32,128]{1,0:T(8,128)S(1)} %copy-done.3, f32[1,128]{1,0:T(1,128)S(1)} %copy-done.4, ...), custom_call_target="tpu_custom_call" | custom-call | tf_op jit(solution)/shard_map/pallas_call | solution.py:557
  91.3 3.1 %copy.24 = f32[1,128,32,128]{3,2,1,0:T(8,128)} copy(f32[1,128,32,128]{3,2,1,0:T(8,128)} %bitcast.26) | data formatting | bytes 4194304
Async XLA Ops:
  2.7 1.0 %copy-start = (f32[4,1,256,128]{3,2,1,0:T(8,128)S(1)}, f32[4,1,256,128]{3,2,1,0:T(8,128)}, u32[]{:S(2)}) copy-start(f32[4,1,256,128]{3,2,1,0:T(8,128)} %param.11) | copy-start | bytes 1572868
  3.8 0.8 copy-start.1
  4.6 0.8 copy-start.2
  5.5 0.7 copy-start.3
  6.2 0.7 copy-start.4
where the time goes:
time: 94.8 us; the launch traced here: 94.4 us
  Pallas kernels  84.5 us (89%)
  local copies, waits for them, and re-layouts  9.91 us (10%)
    pallas_call x1, Pallas kernels, body(): pl.pallas_call(kernel, out_shape=jax.ShapeDtypeStruct((LEV * ROWS, COLS),...  84.5 us
    unnamed x15, local copies, waits for them, and re-layouts  9.91 us

commit v1 on v0

--- a/solution.py
+++ b/solution.py
@@ -40,6 +40,15 @@
 def kernel(
     state_hbm,
     innov_hbm,
+    owner_hbm,
+    column_hbm,
+    coupler_hbm,
+    mask_hbm,
+    diff_hbm,
+    vert_hbm,
+    fout_hbm,
+    fin_hbm,
+    out_hbm,
     owner_ref,
     column_ref,
     coupler_ref,
@@ -48,7 +57,6 @@
     vert_ref,
     fout_ref,
     fin_ref,
-    out_hbm,
     grid_in,
     innov,
     ext,
@@ -74,6 +82,11 @@
     fin_w,
     fin_wt,
     small,
+    edge_row,
+    edge_col,
+    halo_col,
+    edge_flux,
+    halo_flux,
     load_sem,
     s1,
     r1,
@@ -95,16 +108,36 @@
     z = lax.rem(gx, 4) * 2 + gy // 4
     q = x * 4 + y
 
-    load_innov = pltpu.make_async_copy(innov_hbm, innov, load_sem.at[0])
-    load_state = pltpu.make_async_copy(state_hbm, grid_in, load_sem.at[1])
-    load_innov.start()
-    load_state.start()
+    loads = [
+        pltpu.make_async_copy(src, dst, load_sem.at[i])
+        for i, (src, dst) in enumerate(
+            (
+                (owner_hbm, owner_ref),
+                (innov_hbm, innov),
+                (vert_hbm, vert_ref),
+                (fout_hbm, fout_ref),
+                (fin_hbm, fin_ref),
+                (column_hbm, column_ref),
+                (coupler_hbm, coupler_ref),
+                (mask_hbm, mask_ref),
+                (diff_hbm, diff_ref),
+            )
+        )
+    ]
+    for load in loads:
+        load.start()
+
+    def load_row(r, carry):
+        pltpu.make_async_copy(state_hbm.at[:, r, :], grid_in.at[r], out_sem).start()
+        return carry
+
+    lax.fori_loop(0, ROWS, load_row, 0)
 
     def zero_edges(step, carry):
         ext[step, 0] = jnp.zeros((144, LEV), F32)
         ext[step, ROWS + 1] = jnp.zeros((144, LEV), F32)
-        ext[step, 1 : ROWS + 1, 0:8, :] = jnp.zeros((ROWS, 8, LEV), F32)
-        ext[step, 1 : ROWS + 1, 136:144, :] = jnp.zeros((ROWS, 8, LEV), F32)
+        halo_col[step] = jnp.zeros((2, ROWS, LEV), F32)
+        halo_flux[step] = jnp.zeros((2, 8, COLS), F32)
         return carry
 
     lax.fori_loop(0, STEPS, zero_edges, 0)
@@ -140,6 +173,8 @@
     for there, _ in sides:
         greeted = greeted + jnp.where(there, 1, 0)
 
+    for load in loads[2:5]:
+        load.wait()
     vert = vert_ref[...]
     v_high, v_low = halves(vert)
     weights[0:128, 0:128] = v_high
@@ -152,8 +187,9 @@
     weights_t[128:256, 0:128] = vt_low
     weights_t[128:256, 128:256] = vt_low
     small[...] = jnp.zeros((16, LEV), F32)
-    small[0:FIELDS, :] = fout_ref[...]
-    small[8 : 8 + FIELDS, :] = fin_ref[...]
+    for f in range(FIELDS):
+        small[f : f + 1, :] = fout_ref[f]
+        small[8 + f : 9 + f, :] = fin_ref[f]
     flux_w = lax.dot_general(
         small[0:8, :], vert, NT, precision=lax.Precision.HIGHEST, preferred_element_type=F32
     )
@@ -174,7 +210,7 @@
     earlier = sub_b < lane_b
 
     def slot_of(step):
-        owner = owner_ref[pl.ds(step, 1), :]
+        owner = owner_ref[step]
         first, second = owner[:, 0:128], owner[:, 128:256]
         first_b = jnp.broadcast_to(first, (128, 128))
         second_b = jnp.broadcast_to(second, (128, 128))
@@ -205,7 +241,7 @@
         high, low = halves(innov[step])
         placed = dot(placing, jnp.concatenate([high, low], axis=1), NN)
         send_buf[step] = (placed[:, 0:LEV] + placed[:, LEV:]).reshape(16, 32, LEV)
-        columns = column_ref[pl.ds(step, 1), :]
+        columns = column_ref[step]
         to_q = jnp.broadcast_to(owner_q, (16, PROF)) == lax.broadcasted_iota(I32, (16, PROF), 0)
         row_part = jnp.where(to_q, (columns >> 7).astype(F32), 0.0)
         col_part = jnp.where(to_q, (columns & 127).astype(F32), 0.0)
@@ -268,7 +304,8 @@
         ).wait()
         many(prof_buf.at[step, pl.ds(0, 7)], r2.at[step]).wait()
 
-    load_innov.wait()
+    for load in loads[0:2] + loads[5:]:
+        load.wait()
     lines = pack(3)
     pl.semaphore_wait(barrier, greeted)
     first_leg(3)
@@ -293,12 +330,12 @@
     lax.fori_loop(1, 16, send_columns, 0)
     second_leg(3)
 
-    load_state.wait()
+    many(grid_in, out_sem).wait()
 
     def turn(i, carry):
         for u in range(4):
             r = i * 4 + u
-            ext[3, r + 1, 8:136, :] = grid_in[pl.ds(r, LEV, stride=ROWS), :].T
+            ext[3, r + 1, 8:136, :] = grid_in[r].T
         return carry
 
     lax.fori_loop(0, ROWS // 4, turn, 0)
@@ -354,21 +391,45 @@
     def chunk_rows(i):
         return pl.ds(1 + i * HALF, HALF)
 
-    def scatter(step):
+    cell = lax.broadcasted_iota(I32, (COLS, SLOTS), 0).astype(F32).astype(BF)
+
+    def match(first, value, second, count):
+        wanted = jnp.where(first == value, second, -1.0)
+        wanted = jnp.broadcast_to(wanted, (16, SLOTS)).astype(BF)
+        wanted = jnp.concatenate([wanted] * (count // 16), axis=0)
+        return jnp.where(wanted == cell[0:count], BF(1), BF(0))
+
+    def ids(step):
+        return col_rows[0, step : step + 1, :], col_rows[1, step : step + 1, :]
+
+    def row_edges(step):
         high, low = halves(prof_buf[step].reshape(SLOTS, LEV))
         prof_hl[:, 0:LEV] = high
         prof_hl[:, LEV:] = low
-        rows_id = col_rows[0, step : step + 1, :]
-        cols_id = col_rows[1, step : step + 1, :]
-        cell = lax.broadcasted_iota(I32, (COLS, SLOTS), 0).astype(F32).astype(BF)
+        rows_id, cols_id = ids(step)
+        onehot[0:128, :] = match(rows_id, 0.0, cols_id, COLS)
+        onehot[128:256, :] = match(rows_id, float(ROWS - 1), cols_id, COLS)
+        added = dot(onehot[0:256, :], prof_hl[...], NN)
+        added = added[:, 0:LEV] + added[:, LEV:]
+        edge_row[step, 0] = ext[step, 1, 8:136, :] + added[0:128]
+        edge_row[step, 1] = ext[step, ROWS, 8:136, :] + added[128:256]
+
+    def col_edges(step):
+        rows_id, cols_id = ids(step)
+        onehot[0:32, :] = match(cols_id, 0.0, rows_id, ROWS)
+        onehot[32:64, :] = match(cols_id, float(COLS - 1), rows_id, ROWS)
+        added = dot(onehot[0:64, :], prof_hl[...], NN)
+        added = added[:, 0:LEV] + added[:, LEV:]
+        edge_col[step, 0] = ext[step, 1 : ROWS + 1, 8, :] + added[0:32]
+        edge_col[step, 1] = ext[step, 1 : ROWS + 1, 135, :] + added[32:64]
+
+    def scatter(step):
+        rows_id, cols_id = ids(step)
 
         def chunk(i, carry):
             for u in range(HALF):
                 r = (i * HALF + u).astype(F32)
-                wanted = jnp.where(rows_id == r, cols_id, -1.0)
-                wanted = jnp.broadcast_to(wanted, (16, SLOTS)).astype(BF)
-                wanted = jnp.concatenate([wanted] * 8, axis=0)
-                onehot[u * COLS : (u + 1) * COLS, :] = jnp.where(wanted == cell, BF(1), BF(0))
+                onehot[u * COLS : (u + 1) * COLS, :] = match(rows_id, r, cols_id, COLS)
             added = dot(onehot[...], prof_hl[...], NN)
             added = (added[:, 0:LEV] + added[:, LEV:]).reshape(HALF, COLS, LEV)
             ext[step, chunk_rows(i), 8:136, :] = ext[step, chunk_rows(i), 8:136, :] + added
@@ -377,36 +438,46 @@
         lax.fori_loop(0, 2, chunk, 0)
 
     def halo_copy(step, side):
-        row, col = pl.ds(8, COLS), pl.ds(1, ROWS)
         src, dst = (
-            (ext.at[step, 1, row], ext.at[step, ROWS + 1, row]),
-            (ext.at[step, ROWS, row], ext.at[step, 0, row]),
-            (ext.at[step, col, pl.ds(8, 1)], ext.at[step, col, pl.ds(136, 1)]),
-            (ext.at[step, col, pl.ds(135, 1)], ext.at[step, col, pl.ds(7, 1)]),
+            (edge_row.at[step, 0], ext.at[step, ROWS + 1, pl.ds(8, COLS)]),
+            (edge_row.at[step, 1], ext.at[step, 0, pl.ds(8, COLS)]),
+            (edge_col.at[step, 0], halo_col.at[step, 1]),
+            (edge_col.at[step, 1], halo_col.at[step, 0]),
+            (edge_flux.at[step, 0], halo_flux.at[step, 1]),
+            (edge_flux.at[step, 1], halo_flux.at[step, 0]),
         )[side]
         return pltpu.make_async_remote_copy(
             src,
             dst,
             halo_s.at[step, side],
             halo_r.at[step, side],
-            device_id=sides[side][1],
+            device_id=sides[side % 4][1],
             device_id_type=MESH,
         )
 
-    def halo_start(step):
-        for side in range(4):
-
-            @pl.when(sides[side][0])
+    def halo_start(step, which):
+        for side in which:
+
+            @pl.when(sides[side % 4][0])
             def _(side=side):
                 halo_copy(step, side).start()
 
-    def halo_wait(step):
-        for side in range(4):
-
-            @pl.when(sides[side][0])
+    def halo_wait(step, which):
+        for side in which:
+
+            @pl.when(sides[side % 4][0])
             def _(side=side):
                 halo_copy(step, side).wait_send()
                 halo_copy(step, side ^ 1).wait_recv()
+
+    def place_halos(step):
+        ext[step, 1 : ROWS + 1, 7, :] = halo_col[step, 0]
+        ext[step, 1 : ROWS + 1, 136, :] = halo_col[step, 1]
+        if step < 3:
+            value = jnp.concatenate([halo_flux[step, 0], halo_flux[step, 1]], axis=1)
+            added = dot(in_parts(value), fin_w[...], TN)
+            ext[step, 0, 8:136, :] = ext[step, 0, 8:136, :] + added[0:COLS]
+            ext[step, ROWS + 1, 8:136, :] = ext[step, ROWS + 1, 8:136, :] + added[COLS:]
 
     def stencil(step):
         rate = diff_ref[0:1, :]
@@ -463,80 +534,97 @@
 
         lax.fori_loop(0, 2, chunk, 0)
 
+    def couple_block(step, b):
+        index = coupler_ref[step, pl.ds(pl.multiple_of(b * 8, 8), 8), :]
+        lane, row = index & 127, index >> 7
+        sums = [jnp.zeros((8, COLS), F32) for _ in range(FIELDS)]
+        for r in range(ROWS):
+            hit = row == r
+            for f in range(FIELDS):
+                line = jnp.broadcast_to(partner[step, r, f : f + 1, :], (8, COLS))
+                sums[f] = jnp.where(hit, jnp.take_along_axis(line, lane, axis=1), sums[f])
+        for f in range(FIELDS):
+            for j in range(8):
+                received[b * 8 + j, f : f + 1, :] = sums[f][j : j + 1, :]
+
     def couple(step):
         def block(b, carry):
-            index = coupler_ref[step, pl.ds(pl.multiple_of(b * 8, 8), 8), :]
-            lane, row = index & 127, index >> 7
-            sums = [jnp.zeros((8, COLS), F32) for _ in range(FIELDS)]
-            for r in range(ROWS):
-                hit = row == r
-                for f in range(FIELDS):
-                    line = jnp.broadcast_to(partner[step, r, f : f + 1, :], (8, COLS))
-                    sums[f] = jnp.where(hit, jnp.take_along_axis(line, lane, axis=1), sums[f])
-            for f in range(FIELDS):
-                for j in range(8):
-                    received[b * 8 + j, f : f + 1, :] = sums[f][j : j + 1, :]
+            couple_block(step, b)
             return carry
 
         lax.fori_loop(0, 4, block, 0)
 
-    def received_parts(i):
-        value = jnp.concatenate([received[i * HALF + j] for j in range(HALF)], axis=1)
+    def in_parts(value):
         high = value.astype(BF).astype(F32)
         low = value - high
         return jnp.concatenate([high, low, high, low], axis=0).astype(BF)
 
+    def received_parts(first, count):
+        return in_parts(jnp.concatenate([received[first + j] for j in range(count)], axis=1))
+
     def add_fluxes(step):
         def chunk(i, carry):
-            added = dot(received_parts(i), fin_w[...], TN).reshape(HALF, COLS, LEV)
+            added = dot(received_parts(i * HALF, HALF), fin_w[...], TN).reshape(HALF, COLS, LEV)
             ext[step, chunk_rows(i), 8:136, :] = ext[step, chunk_rows(i), 8:136, :] + added
             return carry
 
         lax.fori_loop(0, 2, chunk, 0)
 
-    def finish():
+    def last_vertical():
         def chunk(i, carry):
             mixed = dot(weights_t[...], state_hl[chunk_cells(i), :], NT)
             mixed = mixed[0:LEV] + mixed[LEV:]
-            mixed = mixed + dot(fin_wt[:, 0:32], received_parts(i), NN)
             for j in range(HALF):
-                grid_in[pl.ds(i * HALF + j, LEV, stride=ROWS), :] = mixed[
-                    :, j * COLS : (j + 1) * COLS
-                ]
+                grid_in[i * HALF + j] = mixed[:, j * COLS : (j + 1) * COLS]
             return carry
 
         lax.fori_loop(0, 2, chunk, 0)
+
+    def last_fluxes():
+        def block(b, carry):
+            couple_block(0, b)
+            added = dot(fin_wt[:, 0:32], received_parts(b * 8, 8), NN)
+            for j in range(8):
+                r = b * 8 + j
+                grid_in[r] = grid_in[r] + added[:, j * COLS : (j + 1) * COLS]
+                pltpu.make_async_copy(grid_in.at[r], out_hbm.at[:, r, :], out_sem).start()
+            return carry
+
+        lax.fori_loop(0, 4, block, 0)
 
     for step in (3, 2, 1, 0):
         if step < 3:
             vertical(step)
-        if step == 3:
-            second_leg(1)
         arrived(step)
-        scatter(step)
+        row_edges(step)
+        halo_start(step, (0, 1))
+        if step > 1:
+            second_leg(step - 2)
         if step < 3:
             partner_copy(step + 1).wait()
             couple(step + 1)
+            edge_flux[step, 0] = received[0]
+            edge_flux[step, 1] = received[ROWS - 1]
+            halo_start(step, (4, 5))
             add_fluxes(step)
-        halo_start(step)
-        if step == 3:
-            second_leg(0)
-        halo_wait(step)
+        col_edges(step)
+        halo_start(step, (2, 3))
+        scatter(step)
+        halo_wait(step, (0, 1, 2, 3) if step == 3 else (0, 1, 2, 3, 4, 5))
+        place_halos(step)
         stencil(step)
         surfaces(step)
         partner_copy(step).start()
+    last_vertical()
     partner_copy(0).wait()
-    couple(0)
-    finish()
-    store = pltpu.make_async_copy(grid_in, out_hbm, out_sem)
-    store.start()
+    last_fluxes()
 
     many(col_mid.at[pl.ds(0, 15)], col_sem.at[0]).wait()
     many(col_recv.at[pl.ds(0, 7)], col_sem.at[2]).wait()
     for step in range(STEPS):
         many(mid_buf.at[step, pl.ds(0, 15)], s1.at[step]).wait()
         many(prof_buf.at[step, pl.ds(0, 7)], s2.at[step]).wait()
-    store.wait()
+    many(grid_in, out_sem).wait()
 
 
 def body(
@@ -551,16 +639,23 @@
     flux_out,
     flux_in,
 ):
-    whole = pl.BlockSpec(memory_space=pl.ANY)
-    near = pl.BlockSpec(memory_space=pltpu.VMEM)
+    whole = pl.BlockSpec(memory_space=pltpu.HBM)
     dma = pltpu.SemaphoreType.DMA
     result = pl.pallas_call(
         kernel,
-        out_shape=jax.ShapeDtypeStruct((LEV * ROWS, COLS), F32),
-        in_specs=[whole, whole] + [near] * 8,
+        out_shape=jax.ShapeDtypeStruct((LEV, ROWS, COLS), F32),
+        in_specs=[whole] * 10,
         out_specs=whole,
         scratch_shapes=[
-            pltpu.VMEM((LEV * ROWS, COLS), F32),
+            pltpu.VMEM((STEPS, 1, PROF), I32),
+            pltpu.VMEM((STEPS, 1, PROF), I32),
+            pltpu.VMEM((STEPS, ROWS, COLS), I32),
+            pltpu.VMEM((ROWS, COLS), I32),
+            pltpu.VMEM((1, LEV), F32),
+            pltpu.VMEM((LEV, LEV), F32),
+            pltpu.VMEM((FIELDS, 1, LEV), F32),
+            pltpu.VMEM((FIELDS, 1, LEV), F32),
+            pltpu.VMEM((ROWS, LEV, COLS), F32),
             pltpu.VMEM((STEPS, PROF, LEV), F32),
             pltpu.VMEM((STEPS, ROWS + 2, 144, LEV), F32),
             pltpu.VMEM((STEPS, 16, 32, LEV), F32),
@@ -585,7 +680,12 @@
             pltpu.VMEM((32, LEV), BF),
             pltpu.VMEM((LEV, 128), BF),
             pltpu.VMEM((16, LEV), F32),
-            dma((2,)),
+            pltpu.VMEM((STEPS, 2, COLS, LEV), F32),
+            pltpu.VMEM((STEPS, 2, ROWS, LEV), F32),
+            pltpu.VMEM((STEPS, 2, ROWS, LEV), F32),
+            pltpu.VMEM((STEPS, 2, 8, COLS), F32),
+            pltpu.VMEM((STEPS, 2, 8, COLS), F32),
+            dma((9,)),
             dma((STEPS,)),
             dma((STEPS,)),
             dma((STEPS,)),
@@ -593,26 +693,26 @@
             dma((STEPS,)),
             dma((STEPS,)),
             dma((4,)),
-            dma((STEPS, 4)),
-            dma((STEPS, 4)),
+            dma((STEPS, 6)),
+            dma((STEPS, 6)),
             dma((STEPS,)),
             dma((STEPS,)),
             dma,
         ],
         compiler_params=pltpu.CompilerParams(
-            collective_id=0, has_side_effects=True, vmem_limit_bytes=52 * 2**20
+            collective_id=0, has_side_effects=True, vmem_limit_bytes=64 * 2**20
         ),
     )(
-        final_adjoint.reshape(LEV * ROWS, COLS),
+        final_adjoint.reshape(LEV, ROWS, COLS),
         innovations.reshape(STEPS, PROF, LEV),
-        obs_owner.reshape(STEPS, PROF),
-        obs_column.reshape(STEPS, PROF),
+        obs_owner.reshape(STEPS, 1, PROF),
+        obs_column.reshape(STEPS, 1, PROF),
         coupler.reshape(STEPS, ROWS, COLS),
         sea_mask,
         diffusion,
         vertical[0],
-        flux_out[0],
-        flux_in[0].T,
+        flux_out.reshape(FIELDS, 1, LEV),
+        flux_in[0].T.reshape(FIELDS, 1, LEV),
     )
     return result.reshape(1, LEV, ROWS, COLS)
 

time: 94.8 us -> 81.8 us (0.86)
  Pallas kernels: 84.5 us -> 76.9 us
  local copies, waits for them, and re-layouts: 9.91 us -> 4.35 us
    pallas_call x1, Pallas kernels: 84.5 us -> 76.9 us  [body(): pl.pallas_call(kernel, out_shape=jax.ShapeDtypeStruct((LEV, ROWS, COLS),...]
    unnamed x15 -> x2, local copies, waits for them, and re-layouts: 9.91 us -> 3.76 us
where the time goes in v1:
time: 81.8 us; the launch traced here: 81.3 us
  Pallas kernels  76.9 us (94%)
  local copies, waits for them, and re-layouts  4.35 us (5%)
    pallas_call x1, Pallas kernels, body(): pl.pallas_call(kernel, out_shape=jax.ShapeDtypeStruct((LEV, ROWS, COLS),...  76.9 us
    unnamed x2, local copies, waits for them, and re-layouts  3.76 us

profile of v1, /device:TPU:35, one launch (start us, length us, event | category | flops | bytes accessed | tf_op | source)
XLA Modules:
  0.0 81.3 jit_solution(15425293078066955613)
XLA Ops:
  0.0 0.7 copy.13
  0.7 0.6 reshape.26.fin_hbm
  1.3 76.9 %shard_map.100 = f32[128,32,128]{2,1,0:T(8,128)} custom-call(f32[128,32,128]{2,1,0:T(8,128)} %bitcast.13, f32[4,256,128]{2,1,0:T(8,128)} %bitcast.14, s32[4,1,256]{2,1,0:T(1,128)} %bitcast.18, s32[4,1,256]{2,1,0:T(1,128)} %column_hbm.1, s32[4,32,128]{2,1,0:T(8,128)} %bitcast.15, s32[32,128]{1,0:T(8,128)} %mask_hbm.1, f32[1,128]{1,0:T(1,128)} %diff_hbm.1, ...), custom_call_target="tpu_custom_call" | custom-call | tf_op jit(solution)/shard_map/pallas_call | solution.py:644
  78.2 3.1 %copy.15 = f32[1,128,32,128]{3,2,1,0:T(8,128)} copy(f32[1,128,32,128]{3,2,1,0:T(8,128)} %bitcast.12) | data formatting | bytes 4194304

commit v2 on v1

--- a/solution.py
+++ b/solution.py
@@ -311,7 +311,6 @@
     first_leg(3)
     for step in (2, 1, 0):
         lines = lines + pack(step)
-        first_leg(step)
     col_send[...] = jnp.broadcast_to(lines[:, None, :], (16, 8, LEV))
     col_mid[pl.ds(q, 1)] = col_send[pl.ds(q, 1)]
 
@@ -329,6 +328,7 @@
 
     lax.fori_loop(1, 16, send_columns, 0)
     second_leg(3)
+    first_leg(2)
 
     many(grid_in, out_sem).wait()
 
@@ -358,6 +358,7 @@
 
     lax.fori_loop(1, 8, send_lines, 0)
     second_leg(2)
+    first_leg(1)
 
     is_ocean = comp == 0
 
@@ -598,8 +599,6 @@
         arrived(step)
         row_edges(step)
         halo_start(step, (0, 1))
-        if step > 1:
-            second_leg(step - 2)
         if step < 3:
             partner_copy(step + 1).wait()
             couple(step + 1)
@@ -609,6 +608,10 @@
             add_fluxes(step)
         col_edges(step)
         halo_start(step, (2, 3))
+        if step > 1:
+            second_leg(step - 2)
+            if step == 3:
+                first_leg(0)
         scatter(step)
         halo_wait(step, (0, 1, 2, 3) if step == 3 else (0, 1, 2, 3, 4, 5))
         place_halos(step)

time: 81.8 us -> 73.8 us (0.902)
  the two profiles are of different devices: /device:TPU:35 before, /device:TPU:25 now
where the time goes in v2:
time: 73.8 us; the launch traced here: 73.6 us
  Pallas kernels  69.3 us (94%)
  local copies, waits for them, and re-layouts  4.35 us (6%)
    pallas_call x1, Pallas kernels, body(): pl.pallas_call(kernel, out_shape=jax.ShapeDtypeStruct((LEV, ROWS, COLS),...  69.3 us
    unnamed x2, local copies, waits for them, and re-layouts  3.76 us

profile of v2, /device:TPU:25, one launch (start us, length us, event | category | flops | bytes accessed | tf_op | source)
XLA Modules:
  0.0 73.6 jit_solution(17744994285158329653)
XLA Ops:
  0.0 0.7 copy.13
  0.7 0.6 reshape.26.fin_hbm
  1.3 69.3 %shard_map.100 = f32[128,32,128]{2,1,0:T(8,128)} custom-call(f32[128,32,128]{2,1,0:T(8,128)} %bitcast.13, f32[4,256,128]{2,1,0:T(8,128)} %bitcast.14, s32[4,1,256]{2,1,0:T(1,128)} %bitcast.18, s32[4,1,256]{2,1,0:T(1,128)} %column_hbm.1, s32[4,32,128]{2,1,0:T(8,128)} %bitcast.15, s32[32,128]{1,0:T(8,128)} %mask_hbm.1, f32[1,128]{1,0:T(1,128)} %diff_hbm.1, ...), custom_call_target="tpu_custom_call" | custom-call | tf_op jit(solution)/shard_map/pallas_call | solution.py:647
  70.6 3.1 %copy.15 = f32[1,128,32,128]{3,2,1,0:T(8,128)} copy(f32[1,128,32,128]{3,2,1,0:T(8,128)} %bitcast.12) | data formatting | bytes 4194304
